TPU v7x, 32 devices: a whole 2x2x4 slice. The times are simulated.
32 devices in a mesh: section: 4 (over y, x), ctx: 8 (over z, core).
Axes of the slice: x: 2, y: 2, z: 4, core: 2. Of those that a mesh axis runs over, the one named last changes fastest.
Arguments:
- acts: bfloat16 [4, 1024, 12288], P('section', 'ctx'), may hold values from -6 to 6
- cots: bfloat16 [4, 1024, 4096], P('section', 'ctx'), may hold values from -1.1953125 to 1.1953125
- kern: float32 [4, 7, 12288], P('section'), may hold values from -2 to 2
- filt: bfloat16 [4, 4096, 1024], P('section', 'ctx'), may hold values from -9 to 9
- skip: float32 [4, 4096], P('section'), may hold values from 0.5 to 1.5
Outputs:
- output: bfloat16 [4, 1024, 4096], P('section', 'ctx')
- input_grad: bfloat16 [4, 1024, 12288], P('section', 'ctx')
- kern_grad: float32 [4, 7, 12288], P('section')
- filt_grad: float32 [4, 4096, 1024], P('section', 'ctx')
- skip_grad: float32 [4, 4096], P('section', 'ctx')
All inputs are finite; a program needn't handle non-finite values.
Results may differ from a plain program's by a relative error of at most 0.023.
Values may be sent and summed in bfloat16 or wider, within the bound.
A program may use at most 192 MiB of HBM per device.

v0:
```python
import math

import jax
import jax.numpy as jnp
from jax import lax
from jax.sharding import PartitionSpec as P


def passed_along(value, axis, steps):
    count = lax.axis_size(axis)
    pairs = [(source, (source + steps) % count) for source in range(count)]
    return lax.ppermute(value, axis, pairs)


def from_behind(block, axis, distance):
    devices = range(lax.axis_size(axis))
    route = [(i - distance, i) for i in devices if i - distance in devices]
    return lax.ppermute(block, axis, route)


def factor_length(total):
    best = 2
    for divisor in range(2, math.isqrt(total) + 1):
        if total % divisor == 0 and divisor % 2 == 0:
            best = divisor
    return (best, total // best)


def phases(rows, cols, total):
    left = jnp.arange(rows, dtype=jnp.int32)[:, None]
    right = jnp.arange(cols, dtype=jnp.int32)[None, :]
    return (left * right % total).astype(jnp.float32) * (2.0 * math.pi / total)


def block_table(cos_t, sin_t, sign):
    top = jnp.stack([cos_t, sign * sin_t], axis=1)
    bottom = jnp.stack([-sign * sin_t, cos_t], axis=1)
    return jnp.stack([top, bottom], axis=0)


def make_tables(first, second):
    total = first * second
    outer = phases(first, first // 2, first)
    twist = phases(first, second, total)
    inner = phases(second, second, second)
    outer_pair = jnp.stack([jnp.cos(outer), -jnp.sin(outer)], axis=0)
    inner_cos = jnp.cos(inner)
    inner_sin = jnp.sin(inner)
    return (
        outer_pair,
        jnp.cos(twist),
        jnp.sin(twist),
        block_table(inner_cos, inner_sin, 1.0),
        block_table(inner_cos, inner_sin, -1.0),
    )


def contract(form, table, values):
    return jnp.einsum(form, table, values, precision=lax.Precision.HIGH)


def contract_narrow(form, table, values):
    upper = table.astype(jnp.bfloat16)
    lower = (table - upper.astype(jnp.float32)).astype(jnp.bfloat16)
    return jnp.einsum(form, upper, values, preferred_element_type=jnp.float32) + jnp.einsum(
        form, lower, values, preferred_element_type=jnp.float32
    )


def forward_transform(signal, tables):
    outer_pair, twist_cos, twist_sin, inner_fwd, inner_inv = tables
    first, second = twist_cos.shape
    columns = signal.shape[1]
    blocked = signal.reshape(first // 2, second, columns)
    spread = contract_narrow("pkm,mjc->pkjc", outer_pair, blocked)
    a_real = spread[0]
    a_imag = spread[1]
    b_real = a_real * twist_cos[:, :, None] + a_imag * twist_sin[:, :, None]
    b_imag = a_imag * twist_cos[:, :, None] - a_real * twist_sin[:, :, None]
    stacked = jnp.stack([b_real, b_imag], axis=0)
    return contract("pqsj,skjc->pkqc", inner_fwd, stacked)


def cmul(left, right, conj_right):
    if conj_right:
        return jnp.stack(
            [left[0] * right[0] + left[1] * right[1], left[1] * right[0] - left[0] * right[1]],
            axis=0,
        )
    return jnp.stack(
        [left[0] * right[0] - left[1] * right[1], left[0] * right[1] + left[1] * right[0]], axis=0
    )


def inverse_transform(spectrum, tables):
    outer_pair, twist_cos, twist_sin, inner_fwd, inner_inv = tables
    first, second = twist_cos.shape
    columns = spectrum.shape[3]
    back = contract("pjsq,skqc->pkjc", inner_inv, spectrum)
    g_real = back[0] * twist_cos[:, :, None] - back[1] * twist_sin[:, :, None]
    g_imag = back[0] * twist_sin[:, :, None] + back[1] * twist_cos[:, :, None]
    result = contract("skm,skjc->mjc", outer_pair, jnp.stack([g_real, g_imag], axis=0))
    return result.reshape(first // 2 * second, columns) / (first * second)


def on_device(acts, cots, kern, filt, skip):
    source = passed_along(acts, "section", 1)[0]
    incoming = passed_along(cots, "section", -1)[0]
    taps = kern.shape[1]
    margin = taps - 1
    tokens_dev, feats = source.shape
    width = feats // 3
    groups = lax.axis_size("ctx")
    chans = width // groups
    seq_len = tokens_dev * groups
    before = from_behind(source[tokens_dev - margin :], "ctx", 1)
    padded = jnp.concatenate([before, source], axis=0).astype(jnp.float32)
    weights = kern[0]
    feature = sum(
        (
            weights[offset][None, :] * padded[margin - offset : margin - offset + tokens_dev]
            for offset in range(taps)
        )
    )
    query = feature[:, :width]
    keyed = feature[:, width : 2 * width]
    value = feature[:, 2 * width :]
    gated = (keyed * value).astype(jnp.bfloat16)
    gain_all = skip[0]
    gain_part = lax.dynamic_slice_in_dim(gain_all, lax.axis_index("ctx") * chans, chans)
    first, second = factor_length(2 * seq_len)
    tables = make_tables(first, second)
    filt_spec = forward_transform(filt[0].T, tables)
    grad_in = incoming.astype(jnp.float32)
    grad_mix = (grad_in * query).astype(jnp.bfloat16)
    gated_part = lax.all_to_all(gated, "ctx", split_axis=1, concat_axis=0, tiled=True)
    gated_f = gated_part.astype(jnp.float32)
    gated_spec = forward_transform(gated_part, tables)
    mixed = inverse_transform(cmul(gated_spec, filt_spec, False), tables)
    mixed_part = mixed.astype(jnp.bfloat16)
    mixed_seq = lax.all_to_all(mixed_part, "ctx", split_axis=0, concat_axis=1, tiled=True)
    grad_part = lax.all_to_all(grad_mix, "ctx", split_axis=1, concat_axis=0, tiled=True)
    gated_f, gated_spec = (gated_f, gated_spec)
    grad_f = grad_part.astype(jnp.float32)
    grad_spec = forward_transform(grad_part, tables)
    back = inverse_transform(cmul(grad_spec, filt_spec, True), tables)
    filt_grad = inverse_transform(cmul(grad_spec, gated_spec, True), tables)
    through = (back + gain_part[None, :] * grad_f).astype(jnp.bfloat16)
    skip_grad = jnp.sum(grad_f * gated_f, axis=0)
    through_part, filt_grad, skip_grad = (through, filt_grad, skip_grad)
    through_seq = lax.all_to_all(through_part, "ctx", split_axis=0, concat_axis=1, tiled=True)
    inner = mixed_seq.astype(jnp.float32) + gain_all[None, :] * gated.astype(jnp.float32)
    output = (query * inner).astype(jnp.bfloat16)
    through_f = through_seq.astype(jnp.float32)
    feat_grad = jnp.concatenate([grad_in * inner, through_f * value, through_f * keyed], axis=1)
    after = from_behind(feat_grad[:margin].astype(jnp.bfloat16), "ctx", -1).astype(jnp.float32)
    extended = jnp.concatenate([feat_grad, after], axis=0)
    input_grad = sum(
        (
            weights[offset][None, :] * extended[offset : offset + tokens_dev]
            for offset in range(taps)
        )
    ).astype(jnp.bfloat16)
    partial_kern = jnp.sum(
        jnp.stack(
            [
                feat_grad * padded[margin - offset : margin - offset + tokens_dev]
                for offset in range(taps)
            ],
            axis=0,
        ),
        axis=1,
    )
    kern_grad = lax.psum(partial_kern.astype(jnp.bfloat16), "ctx").astype(jnp.float32)
    return (output[None], input_grad[None], kern_grad[None], filt_grad.T[None], skip_grad[None])


def solution(mesh):
    return jax.shard_map(
        on_device,
        mesh=mesh,
        in_specs=(
            P("section", "ctx", None),
            P("section", "ctx", None),
            P("section", None, None),
            P("section", "ctx", None),
            P("section", None),
        ),
        out_specs=(
            P("section", "ctx", None),
            P("section", "ctx", None),
            P("section", None, None),
            P("section", "ctx", None),
            P("section", "ctx"),
        ),
        check_vma=False,
    )
```

profile of v0, /device:TPU:0, one launch (start us, length us, event | category | flops | bytes accessed | tf_op | source)
XLA Modules:
  0.0 615.7 jit_solution(11385100000286422987)
XLA Ops:
  18.0 66.9 %collective-permute-done = bf16[1,128,12288]{1,2,0:T(8,128)(2,1)S(1)} collective-permute-done((bf16[1,128,12288]{1,2,0:T(8,128)(2,1)}, bf16[1,128,12288]{1,2,0:T(8,128)(2,1)S(1)}, u32[]{:S(2)}, u32[]{:S(2)}) %collective-permute-start) | collective-permute-done | bytes 3145760 | tf_op jit(solution)/shard_map/ppermute | solution.py:12
  101.7 24.5 %multiply_add_fusion = f32[128,12288]{0,1:T(8,128)} fusion(f32[134,12288]{0,1:T(8,128)S(1)} %maximum_convert_fusion, f32[12288]{0:T(1024)S(1)} %bitcast.243, f32[12288]{0:T(1024)S(1)} %bitcast.245, f32[12288]{0:T(1024)S(1)} %bitcast.235, f32[12288]{0:T(1024)S(1)} %bitcast.237, f32[12288]{0:T(1024)S(1)} %bitcast.239, f32[12288]{0:T(1024)S(1)} %bitcast.241, ...), kind=kLoop, calls=%fused_computation.60 | loop fusion | flops 20447232 | bytes 50675712 | tf_op jit(solution)/shard_map/add | solution.py:119
  129.3 9.6 %all-to-all-start.2 = ((bf16[128,8,512]{0,2,1:T(8,128)(2,1)}), bf16[128,8,512]{0,2,1:T(8,128)(2,1)S(1)}, u32[]{:S(2)}, u32[]{:S(2)}) async-start(bf16[128,8,512]{0,2,1:T(8,128)(2,1)} %bitcast.58), calls=%async_computation.2 | async-start | bytes 2097152 | tf_op jit(solution)/shard_map/all_to_all | solution.py:142
  146.0 19.6 %all-to-all-done.2 = bf16[128,8,512]{0,2,1:T(8,128)(2,1)S(1)} async-done(((bf16[128,8,512]{0,2,1:T(8,128)(2,1)}), bf16[128,8,512]{0,2,1:T(8,128)(2,1)S(1)}, u32[]{:S(2)}, u32[]{:S(2)}) %all-to-all-start.2) | async-done | bytes 1048608 | tf_op jit(solution)/shard_map/all_to_all | solution.py:142
  183.8 9.0 %fusion.40 = f32[2,32,64,512]{3,2,0,1:T(8,128)S(1)} fusion(f32[2,32,64,512,1]{3,1,2,0,4:T(8,128)S(1)} %maximum_bitcast_fusion.4, f32[1,64,2,64]{3,1,2,0:T(8,128)S(1)} %get-tuple-element.57, f32[1,64,2,64]{3,1,2,0:T(8,128)S(1)} %get-tuple-element.60), kind=kOutput, calls=%fused_computation.84 | convolution fusion | flops 1610629120 | bytes 16842752 | tf_op jit(solution)/shard_map/pqsj,skjc->pkqc/dot_general | solution.py:59
  192.8 9.4 %fusion.37 = f32[2,32,64,512]{3,2,0,1:T(8,128)S(1)} fusion(f32[2,32,64,512,1]{3,1,2,0,4:T(8,128)S(1)} %maximum_bitcast_fusion.1, f32[1,64,2,64]{3,1,2,0:T(8,128)S(1)} %get-tuple-element.57, f32[1,64,2,64]{3,1,2,0:T(8,128)S(1)} %get-tuple-element.60), kind=kOutput, calls=%fused_computation.83 | convolution fusion | flops 1610629120 | bytes 16842752 | tf_op jit(solution)/shard_map/pqsj,skjc->pkqc/dot_general | solution.py:59
  227.0 29.0 %all_to_all.52 = bf16[8,128,512]{1,2,0:T(8,128)(2,1)S(1)} all-to-all(bf16[8,128,512]{1,2,0:T(8,128)(2,1)S(1)} %fusion.48), channel_id=1, replica_groups=mesh['section'=4,'ctx'=8] {'ctx'}, dimensions={0} | all-to-all | bytes 2097152 | tf_op jit(solution)/shard_map/all_to_all | solution.py:151
  261.0 29.9 %all_to_all.53 = bf16[128,8,512]{0,2,1:T(8,128)(2,1)} all-to-all(bf16[128,8,512]{0,2,1:T(8,128)(2,1)S(1)} %bitcast.221), channel_id=1, replica_groups=mesh['section'=4,'ctx'=8] {'ctx'}, dimensions={1} | all-to-all | bytes 2097152 | tf_op jit(solution)/shard_map/all_to_all | solution.py:136
  302.9 14.0 %fusion.34 = f32[2,32,64,512]{3,2,0,1:T(8,128)} fusion(f32[2,32,64,512,1]{3,1,2,0,4:T(8,128)} %maximum_bitcast_fusion, f32[1,64,2,64]{3,1,2,0:T(8,128)S(1)} %get-tuple-element.57, f32[1,64,2,64]{3,1,2,0:T(8,128)S(1)} %get-tuple-element.60), kind=kOutput, calls=%fused_computation.82 | convolution fusion | flops 1610629120 | bytes 16842752 | tf_op jit(solution)/shard_map/pqsj,skjc->pkqc/dot_general | solution.py:59
  316.9 12.2 %multiply_add_fusion.2 = (f32[1,32,64,512]{3,2,0,1:T(8,128)}, f32[1,32,64,512]{3,2,0,1:T(8,128)}, f32[1,32,64,512]{3,2,0,1:T(8,128)}, f32[1,32,64,512]{3,2,0,1:T(8,128)}) fusion(f32[2,32,64,512]{3,2,0,1:T(8,128)S(1)} %bitcast.212, f32[2,32,64,512]{3,2,0,1:T(8,128)} %fusion.34, f32[2,32,64,512]{3,2,0,1:T(8,128)} %copy-done.8), kind=kLoop, calls=%fused_computation.64 | loop fusion | flops 12582912 | bytes 41943040 | tf_op jit(solution)/shard_map/add | solution.py:87
  329.1 7.4 %fusion.45 = f32[32,512,2,64]{1,3,2,0:T(8,128)S(1)} fusion(f32[1,32,64,512]{3,2,0,1:T(8,128)} %get-tuple-element.38, f32[1,32,64,512]{3,2,0,1:T(8,128)} %get-tuple-element.39, f32[1,64,2,64]{3,1,2,0:T(8,128)S(1)} %get-tuple-element.61, f32[1,64,2,64]{3,1,2,0:T(8,128)S(1)} %get-tuple-element.56), kind=kOutput, calls=%fused_computation.87 | convolution fusion | flops 1612726272 | bytes 16842752 | tf_op jit(solution)/shard_map/pjsq,skqc->pkjc/dot_general | solution.py:59
  348.5 8.2 %copy.163 = f32[32,512,2,64]{1,0,3,2:T(8,128)} copy(f32[32,512,2,64]{1,3,2,0:T(8,128)S(1)} %fusion.43) | data formatting | bytes 16777216 | tf_op jit(solution)/shard_map/pjsq,skqc->pkjc/dot_general | solution.py:59
  373.9 24.4 %all-to-all-done.1 = bf16[8,128,512]{2,1,0:T(8,128)(2,1)} async-done(((bf16[8,128,512]{2,1,0:T(8,128)(2,1)}), bf16[8,128,512]{2,1,0:T(8,128)(2,1)}, u32[]{:S(2)}, u32[]{:S(2)}) %all-to-all-start.1) | async-done | bytes 1048608 | tf_op jit(solution)/shard_map/all_to_all | solution.py:141
  414.7 10.1 %bitcast_dynamic-update-slice_fusion.6 = f32[7,128,12288]{1,2,0:T(8,128)} fusion(f32[134,12288]{0,1:T(8,128)} %copy-done, f32[128,4096]{0,1:T(8,128)S(1)} %copy-done.1, f32[128,4096]{0,1:T(8,128)S(1)} %get-tuple-element.40, f32[128,4096]{0,1:T(8,128)S(1)} %get-tuple-element.43), kind=kLoop, calls=%fused_computation.59 | loop fusion | flops 4718591 | bytes 18874368
  430.2 10.1 %bitcast_dynamic-update-slice_fusion.5 = f32[7,128,12288]{1,2,0:T(8,128)} fusion(f32[7,128,12288]{1,2,0:T(8,128)} %bitcast_dynamic-update-slice_fusion.6, f32[134,12288]{0,1:T(8,128)} %copy-done, f32[128,4096]{0,1:T(8,128)} %get-tuple-element.41, f32[128,4096]{0,1:T(8,128)S(1)} %get-tuple-element.40, f32[128,4096]{0,1:T(8,128)} %copy-done.4), kind=kLoop, calls=%fused_computation.58 | loop fusion | flops 4718592 | bytes 18874368
  440.4 10.3 %bitcast_dynamic-update-slice_fusion.4 = f32[7,128,12288]{1,2,0:T(8,128)} fusion(f32[7,128,12288]{1,2,0:T(8,128)} %bitcast_dynamic-update-slice_fusion.5, f32[134,12288]{0,1:T(8,128)} %copy-done, f32[128,4096]{0,1:T(8,128)S(1)} %copy-done.2, f32[128,4096]{0,1:T(8,128)S(1)} %get-tuple-element.40, f32[128,4096]{0,1:T(8,128)S(1)} %copy-done.5), kind=kLoop, calls=%fused_computation.57 | loop fusion | flops 4718592 | bytes 18874368
  450.7 7.3 %bitcast_dynamic-update-slice_fusion.3 = f32[7,128,12288]{1,2,0:T(8,128)} fusion(f32[7,128,12288]{1,2,0:T(8,128)} %bitcast_dynamic-update-slice_fusion.4, f32[134,12288]{0,1:T(8,128)S(1)} %bitcast.210, f32[128,4096]{0,1:T(8,128)S(1)} %copy-done.2, f32[128,4096]{0,1:T(8,128)S(1)} %get-tuple-element.40, f32[128,4096]{0,1:T(8,128)S(1)} %copy-done.5), kind=kLoop, calls=%fused_computation.56 | loop fusion | flops 4718592 | bytes 18874368
  458.1 7.3 %bitcast_dynamic-update-slice_fusion.2 = f32[7,128,12288]{1,2,0:T(8,128)} fusion(f32[7,128,12288]{1,2,0:T(8,128)} %bitcast_dynamic-update-slice_fusion.3, f32[134,12288]{0,1:T(8,128)S(1)} %bitcast.210, f32[128,4096]{0,1:T(8,128)S(1)} %copy-done.2, f32[128,4096]{0,1:T(8,128)S(1)} %get-tuple-element.40, f32[128,4096]{0,1:T(8,128)S(1)} %copy-done.5), kind=kLoop, calls=%fused_computation.55 | loop fusion | flops 4718592 | bytes 18874368
  465.4 7.5 %bitcast_dynamic-update-slice_fusion.1 = f32[7,128,12288]{1,2,0:T(8,128)} fusion(f32[7,128,12288]{1,2,0:T(8,128)} %bitcast_dynamic-update-slice_fusion.2, f32[134,12288]{0,1:T(8,128)S(1)} %bitcast.210, f32[128,4096]{0,1:T(8,128)S(1)} %copy-done.2, f32[128,4096]{0,1:T(8,128)S(1)} %get-tuple-element.40, f32[128,4096]{0,1:T(8,128)S(1)} %copy-done.5), kind=kLoop, calls=%fused_computation.54 | loop fusion | flops 4718592 | bytes 18874368
  472.9 7.2 %bitcast_dynamic-update-slice_fusion = f32[7,128,12288]{1,2,0:T(8,128)} fusion(f32[7,128,12288]{1,2,0:T(8,128)} %bitcast_dynamic-update-slice_fusion.1, f32[134,12288]{0,1:T(8,128)S(1)} %bitcast.210, f32[128,4096]{0,1:T(8,128)S(1)} %copy-done.2, f32[128,4096]{0,1:T(8,128)S(1)} %get-tuple-element.40, f32[128,4096]{0,1:T(8,128)S(1)} %copy-done.5), kind=kLoop, calls=%fused_computation.53 | loop fusion | flops 4718592 | bytes 18874368 | tf_op jit(solution)/shard_map/stack | solution.py:165
  480.1 20.5 %reduce_sum.18 = bf16[7,12288]{1,0:T(8,128)(2,1)S(1)} reduce(f32[7,128,12288]{1,2,0:T(8,128)} %bitcast_dynamic-update-slice_fusion, f32[]{:T(128)} %constant.67.clone.1), dimensions={1}, to_apply=%region_0.1 | reduce | flops 10924032 | bytes 44212228 | tf_op jit(solution)/shard_map/reduce_sum | solution.py:164
  513.2 40.4 %all-reduce.2.cloned.1.call-done = bf16[1,7,12288]{2,0,1:T(2,128)(2,1)} async-done(((bf16[1,7,12288]{2,0,1:T(2,128)(2,1)}), bf16[1,7,12288]{2,0,1:T(2,128)(2,1)}) %all-reduce.2.cloned.1.call-update) | async-done | bytes 172048 | tf_op jit(solution)/shard_map/psum | solution.py:174
  559.3 12.5 %pad_maximum_fusion = f32[134,12288]{0,1:T(8,128)} fusion(f32[6,12288]{0,1:T(8,128)} %copy.94, f32[128,4096]{0,1:T(8,128)} %get-tuple-element.41, f32[128,4096]{0,1:T(8,128)S(1)} %get-tuple-element.40, f32[128,4096]{0,1:T(8,128)} %copy-done.4), kind=kLoop, calls=%fused_computation | loop fusion | flops 4939776 | bytes 13172736 | tf_op jit(solution)/shard_map/concatenate | solution.py:157
  571.8 32.2 %fusion.46 = bf16[1,128,12288]{1,2,0:T(8,128)(2,1)} fusion(f32[134,12288]{0,1:T(8,128)} %pad_maximum_fusion, f32[12288]{0:T(1024)S(1)} %bitcast.244, f32[12288]{0:T(1024)S(1)} %bitcast.246, f32[12288]{0:T(1024)S(1)} %bitcast.236, f32[12288]{0:T(1024)S(1)} %bitcast.238, f32[12288]{0:T(1024)S(1)} %bitcast.240, f32[12288]{0:T(1024)S(1)} %bitcast.242, ...), kind=kLoop, calls=%fused_computation.89 | loop fusion | flops 25165824 | bytes 47529984 | tf_op jit(solution)/shard_map/broadcast_in_dim | solution.py:175
  (141 shorter events, 171.3 us)
Async XLA Ops:
  11.8 73.0 %collective-permute-start = (bf16[1,128,12288]{1,2,0:T(8,128)(2,1)}, bf16[1,128,12288]{1,2,0:T(8,128)(2,1)S(1)}, u32[]{:S(2)}, u32[]{:S(2)}) collective-permute-start(bf16[1,128,12288]{1,2,0:T(8,128)(2,1)} %copy.69), channel_id=1, source_target_pairs={{0,8},{8,16},{16,24},{24,0},{1,9},{9,17},{17,25},{25,1},{2,10},{10... | collective-permute-start | bytes 9437192 | tf_op jit(solution)/shard_map/ppermute | solution.py:12
  17.0 109.2 %collective-permute-start.2 = (bf16[1,128,4096]{1,2,0:T(8,128)(2,1)}, bf16[1,128,4096]{1,2,0:T(8,128)(2,1)}, u32[]{:S(2)}, u32[]{:S(2)}) collective-permute-start(bf16[1,128,4096]{1,2,0:T(8,128)(2,1)} %copy.84), channel_id=1, source_target_pairs={{0,24},{8,0},{16,8},{24,16},{1,25},{9,1},{17,9},{25,17},{2,26},{10... | collective-permute-start | bytes 3145736 | tf_op jit(solution)/shard_map/ppermute | solution.py:12
  90.9 3.0 collective-permute-start.1
  101.6 24.6 %copy-start = (f32[134,12288]{0,1:T(8,128)}, f32[134,12288]{0,1:T(8,128)S(1)}, u32[]{:S(2)}) copy-start(f32[134,12288]{0,1:T(8,128)S(1)} %maximum_convert_fusion) | copy-start | bytes 19759108
  126.2 12.8 %copy-start.13 = (bf16[1,512,1024]{2,1,0:T(8,128)(2,1)S(1)}, bf16[1,512,1024]{2,1,0:T(8,128)(2,1)}, u32[]{:S(2)}) copy-start(bf16[1,512,1024]{2,1,0:T(8,128)(2,1)} %param.8) | copy-start | bytes 3145732
  126.2 13.3 %copy-start.28 = (f32[1,4096]{1,0:T(1,128)S(1)}, f32[1,4096]{1,0:T(1,128)}, u32[]{:S(2)}) copy-start(f32[1,4096]{1,0:T(1,128)} %param.9) | copy-start | bytes 49156
  129.3 36.2 %all-to-all-start.2 = ((bf16[128,8,512]{0,2,1:T(8,128)(2,1)}), bf16[128,8,512]{0,2,1:T(8,128)(2,1)S(1)}, u32[]{:S(2)}, u32[]{:S(2)}) async-start(bf16[128,8,512]{0,2,1:T(8,128)(2,1)} %bitcast.58), calls=%async_computation.2 | async-start | bytes 2097152 | tf_op jit(solution)/shard_map/all_to_all | solution.py:142
  298.2 18.8 %slice-start.3 = ((s8[8388608]{0:T(1024)(128)(4,1)}), s8[4194304]{0:T(1024)(128)(4,1)S(1)}, s32[]{:S(2)}) async-start(s8[8388608]{0:T(1024)(128)(4,1)} %bitcast.211), calls=%async_computation.8 | async-start | bytes 8388608
  302.9 14.0 %slice-start.4 = ((s8[8388608]{0:T(1024)(128)(4,1)}), s8[4194304]{0:T(1024)(128)(4,1)S(1)}, s32[]{:S(2)}) async-start(s8[8388608]{0:T(1024)(128)(4,1)} %bitcast.211), calls=%async_computation.9 | async-start | bytes 8388608
  367.5 30.8 %all-to-all-start.1 = ((bf16[8,128,512]{2,1,0:T(8,128)(2,1)}), bf16[8,128,512]{2,1,0:T(8,128)(2,1)}, u32[]{:S(2)}, u32[]{:S(2)}) async-start(bf16[8,128,512]{2,1,0:T(8,128)(2,1)} %bitcast.232), calls=%async_computation.1 | async-start | bytes 2097152 | tf_op jit(solution)/shard_map/all_to_all | solution.py:141
  371.7 181.9 %all-reduce.2.cloned.1.call-start = ((), (), s32[]{:S(2)}) async-start(), calls=%async_computation.4 | async-start | bytes 688128 | tf_op jit(solution)/shard_map/psum | solution.py:174
  373.9 30.3 %copy-start.10 = (bf16[128,4096]{0,1:T(8,128)(2,1)S(1)}, bf16[128,4096]{0,1:T(8,128)(2,1)}, u32[]{:S(2)}) copy-start(bf16[128,4096]{0,1:T(8,128)(2,1)} %copy-done.9) | copy-start | bytes 3145732
  408.0 16.8 %copy-start.4 = (f32[128,4096]{0,1:T(8,128)}, f32[128,4096]{0,1:T(8,128)S(1)}, u32[]{:S(2)}) copy-start(f32[128,4096]{0,1:T(8,128)S(1)} %get-tuple-element.43) | copy-start | bytes 6291460
  428.7 127.0 %collective-permute-start.3 = (bf16[6,12288]{1,0:T(8,128)(2,1)}, bf16[6,12288]{1,0:T(8,128)(2,1)S(1)}, u32[]{:S(2)}, u32[]{:S(2)}) collective-permute-start(bf16[6,12288]{1,0:T(8,128)(2,1)} %copy.93), channel_id=1, source_target_pairs={{1,0},{2,1},{3,2},{4,3},{5,4},{6,5},{7,6},{9,8},{10,9},{11,10},{12... | collective-permute-start | bytes 442376 | tf_op jit(solution)/shard_map/ppermute | solution.py:18
  430.2 20.5 %slice-start = ((s8[12582912]{0:T(1024)(128)(4,1)}), s8[4194304]{0:T(1024)(128)(4,1)S(1)}, s32[]{:S(2)}) async-start(s8[12582912]{0:T(1024)(128)(4,1)} %bitcast.209), calls=%async_computation.5 | async-start | bytes 8388608
  430.2 20.5 %slice-start.1 = ((s8[12582912]{0:T(1024)(128)(4,1)}), s8[4194304]{0:T(1024)(128)(4,1)S(1)}, s32[]{:S(2)}) async-start(s8[12582912]{0:T(1024)(128)(4,1)} %bitcast.209), calls=%async_computation.6 | async-start | bytes 8388608
  559.2 12.5 %copy-start.6 = (f32[128,4096]{0,1:T(8,128)S(1)}, f32[128,4096]{0,1:T(8,128)}, u32[]{:S(2)}) copy-start(f32[128,4096]{0,1:T(8,128)} %copy-done.4) | copy-start | bytes 6291460
  559.2 12.5 %copy-start.15 = (f32[1,1,12288]{2,0,1:T(1,128)S(1)}, f32[1,1,12288]{2,0,1:T(1,128)}, u32[]{:S(2)}) copy-start(f32[1,1,12288]{2,0,1:T(1,128)} %copy-done.14) | copy-start | bytes 147460
  559.2 12.5 %copy-start.17 = (f32[1,1,12288]{2,0,1:T(1,128)S(1)}, f32[1,1,12288]{2,0,1:T(1,128)}, u32[]{:S(2)}) copy-start(f32[1,1,12288]{2,0,1:T(1,128)} %copy-done.16) | copy-start | bytes 147460
  559.2 12.6 %copy-start.19 = (f32[1,1,12288]{2,0,1:T(1,128)S(1)}, f32[1,1,12288]{2,0,1:T(1,128)}, u32[]{:S(2)}) copy-start(f32[1,1,12288]{2,0,1:T(1,128)} %copy-done.18) | copy-start | bytes 147460
  559.2 12.6 %copy-start.21 = (f32[1,1,12288]{2,0,1:T(1,128)S(1)}, f32[1,1,12288]{2,0,1:T(1,128)}, u32[]{:S(2)}) copy-start(f32[1,1,12288]{2,0,1:T(1,128)} %copy-done.20) | copy-start | bytes 147460
  559.2 12.6 %copy-start.23 = (f32[1,1,12288]{2,0,1:T(1,128)S(1)}, f32[1,1,12288]{2,0,1:T(1,128)}, u32[]{:S(2)}) copy-start(f32[1,1,12288]{2,0,1:T(1,128)} %copy-done.22) | copy-start | bytes 147460
  559.2 12.6 %copy-start.25 = (f32[1,1,12288]{2,0,1:T(1,128)S(1)}, f32[1,1,12288]{2,0,1:T(1,128)}, u32[]{:S(2)}) copy-start(f32[1,1,12288]{2,0,1:T(1,128)} %copy-done.24) | copy-start | bytes 147460
  559.2 12.6 %copy-start.27 = (f32[1,1,12288]{2,0,1:T(1,128)S(1)}, f32[1,1,12288]{2,0,1:T(1,128)}, u32[]{:S(2)}) copy-start(f32[1,1,12288]{2,0,1:T(1,128)} %copy-done.26) | copy-start | bytes 147460
  (19 other events, 133.1 us)
Sparse Core Ops, SparseCore 0:
  501.6 51.9 all-reduce.1
where the time goes:
time: 625 us; the launch traced here: 616 us
  other arithmetic  223 us (36%)
  waiting for transfers between devices  151 us (24%)
  matrix products  76 us (12%)
  local copies, waits for them, and re-layouts  70.3 us (11%)
  blocking collectives  58.9 us (9%)
  starting transfers between devices  21.3 us (3%)
  between operations  14.9 us (2%)
    ppermute x2, waiting for transfers between devices, passed_along(): return lax.ppermute(value, axis, pairs)  66.9 us
    dot_general x9, matrix products, contract(): return jnp.einsum(form, table, values, precision=lax.Precision.HIGH)  63.6 us
    unnamed x9, other arithmetic  52.7 us
    psum x1, waiting for transfers between devices, on_device(): lax.psum(partial_kern.astype(jnp.bfloat16), 'ctx').astype(jnp.float32)  40.4 us
    broadcast_in_dim x1, other arithmetic, on_device(): input_grad[None]  32.2 us
    all_to_all x1, blocking collectives, on_device(): lax.all_to_all(gated, 'ctx', split_axis=1, concat_axis=0, tiled=True)  29.9 us
    all_to_all x1, blocking collectives, on_device(): lax.all_to_all(through_part, 'ctx', split_axis=0, concat_axis=1, tiled=True)  29 us
    add x1, other arithmetic, on_device(): sum((weights[offset][None, :] * padded[margin - offset:margin - offset +...  24.5 us
  transfers between devices with their start and end apart: 7, of which 4 were waited for; matrix products, arithmetic and copies ran while one was open for 22% of the time, Pallas kernels for 0%

commit v1 on v0

v1 whole, which is shorter than its diff:
```python
import functools

import jax
import jax.numpy as jnp
import ml_dtypes
import numpy as np
from jax import lax
from jax.experimental import pallas as pl
from jax.experimental.pallas import tpu as pltpu
from jax.sharding import PartitionSpec as P

MESH = pl.DeviceIdType.MESH
LANES = 128
HALO = 16
F32 = jnp.float32
BF16 = jnp.bfloat16


def make_tables(length):
    half = 2 * np.arange(length, dtype=np.int64) + 1
    angle = (np.outer(half, half) % (8 * length)) * (2.0 * np.pi / (8 * length))
    phase = half * (np.pi / (4 * length))
    twist = np.stack([np.cos(phase), np.sin(phase)]).astype(np.float32)
    twist = np.ascontiguousarray(np.broadcast_to(twist[:, :, None], (2, length, LANES)))
    return (
        np.cos(angle).astype(ml_dtypes.bfloat16),
        np.sin(angle).astype(ml_dtypes.bfloat16),
        twist,
    )


def kernel(
    sections, groups, chunks,
    acts, cots, kern, filt, skip, c4, s4, twist,
    out, igrad, kgrad, fgrad, sgrad,
    srcv, incv, hst, hrx, gst, grx, stg, gx, rx, xf, fgb, fsp, prod, kst, krx, ksum, kall,
    src_send, src_recv, inc_send, inc_recv, h_send, h_recv, g_send, g_recv,
    x_send, x_recv, r_send, r_recv, ks_send, ks_recv, ka_send, ka_recv, o_sem, i_sem,
):
    sec = lax.axis_index("section")
    me = lax.axis_index("ctx")
    tokens, width = cots.shape
    chans = width // groups
    taps = kern.shape[0]
    length = c4.shape[0]
    rows_step = 256
    after_sec = lax.rem(sec + 1, sections)
    before_sec = lax.rem(sec + sections - 1, sections)

    barrier = pltpu.get_barrier_semaphore()
    pl.semaphore_signal(barrier, inc=1, device_id={"section": after_sec}, device_id_type=MESH)
    pl.semaphore_signal(barrier, inc=1, device_id={"section": before_sec}, device_id_type=MESH)
    for step in range(1, groups):
        pl.semaphore_signal(
            barrier, inc=1, device_id={"ctx": lax.rem(me + step, groups)}, device_id_type=MESH
        )
    pl.semaphore_wait(barrier, groups + 1)

    def column(part, group, k):
        return pl.multiple_of(part * width + group * chans + k * LANES, LANES)

    def remote(src, dst, send, recv, where):
        return pltpu.make_async_remote_copy(
            src_ref=src, dst_ref=dst, send_sem=send, recv_sem=recv,
            device_id=where, device_id_type=MESH,
        )

    def drain(ref, sem):
        pltpu.make_async_copy(ref, ref, sem).wait()

    def hand_on(k):
        def body(group, carry):
            for part in range(3):
                remote(
                    acts.at[:, pl.ds(column(part, group, k), LANES)],
                    srcv.at[k, part * groups + group],
                    src_send.at[k], src_recv.at[k], {"section": after_sec},
                ).start()
            remote(
                cots.at[:, pl.ds(column(0, group, k), LANES)],
                incv.at[k, group],
                inc_send.at[k], inc_recv.at[k], {"section": before_sec},
            ).start()
            return carry

        lax.fori_loop(0, groups, body, 0)

    def to_peers(make):
        def body(step, carry):
            make(lax.rem(me + step, groups)).start()
            return carry

        lax.fori_loop(1, groups, body, 0)

    def features(k, group):
        result = []
        for part in range(3):
            strip = part * groups + group
            xf[part, :HALO, :] = hrx[k, strip].astype(F32)
            xf[part, HALO:, :] = srcv[k, strip].astype(F32)
            columns = pl.ds(column(part, group, k), LANES)
            total = None
            for j in range(taps):
                term = kern[j : j + 1, columns] * xf[part, pl.ds(HALO - j, tokens), :]
                total = term if total is None else total + term
            result.append(total)
        return result

    hand_on(0)
    if chunks > 1:
        hand_on(1)

    @pl.loop(0, length // rows_step)
    def _(r):
        rows = pl.ds(pl.multiple_of(r * rows_step, rows_step), rows_step)
        dims = (((1,), (1,)), ((), ()))
        c = lax.dot_general(c4[rows, :], filt[...], dims, preferred_element_type=F32)
        s = lax.dot_general(s4[rows, :], filt[...], dims, preferred_element_type=F32)
        tc = twist[0, rows, :]
        ts = twist[1, rows, :]
        for k in range(chunks):
            ck = c[:, k * LANES : (k + 1) * LANES]
            sk = s[:, k * LANES : (k + 1) * LANES]
            fsp[0, k, rows, :] = (ck * tc + sk * ts).astype(BF16)
            fsp[1, k, rows, :] = (sk * tc - ck * ts).astype(BF16)

    def stage_a(k):
        drain(srcv.at[k], src_recv.at[k])
        if k + 2 < chunks:
            drain(srcv.at[k], src_send.at[k])
            drain(incv.at[k], inc_send.at[k])
            hand_on(k + 2)

        @pl.loop(0, 3 * groups)
        def _(strip):
            hst[k, strip] = srcv[k, strip, tokens - HALO :, :]

        @pl.when(me < groups - 1)
        def _():
            remote(hst.at[k], hrx.at[k], h_send.at[k], h_recv.at[k], {"ctx": me + 1}).start()

        drain(incv.at[k], inc_recv.at[k])

        @pl.when(me > 0)
        def _():
            drain(hrx.at[k], h_recv.at[k])

        @pl.when(me == 0)
        def _():
            hrx[k] = jnp.zeros(hrx.shape[1:], BF16)

        @pl.loop(0, groups)
        def _(group):
            query, keyed, value = features(k, group)
            stg[k, group, :, :LANES] = (keyed * value).astype(BF16)
            stg[k, group, :, LANES:] = (incv[k, group].astype(F32) * query).astype(BF16)

        mine = pl.ds(pl.multiple_of(me * tokens, tokens), tokens)
        to_peers(
            lambda peer: remote(
                stg.at[k, peer], gx.at[k, mine, :], x_send.at[k], x_recv.at[k], {"ctx": peer}
            )
        )
        gx[k, mine, :] = stg[k, me]

    def stage_c(k):
        drain(gx.at[k, pl.ds(0, (groups - 1) * tokens), :], x_recv.at[k])

        @pl.loop(0, length // rows_step)
        def _(r):
            rows = pl.ds(pl.multiple_of(r * rows_step, rows_step), rows_step)
            x = gx[k]
            c = jnp.dot(c4[rows, :], x, preferred_element_type=F32)
            s = jnp.dot(s4[rows, :], x, preferred_element_type=F32)
            cg, cm = c[:, :LANES], c[:, LANES:]
            sg, sm = s[:, :LANES], s[:, LANES:]
            fc = fsp[0, k, rows, :].astype(F32)
            fs = fsp[1, k, rows, :].astype(F32)
            prod[0, rows, :LANES] = (cg * fc - sg * fs).astype(BF16)
            prod[1, rows, :LANES] = (cg * fs + sg * fc).astype(BF16)
            prod[0, rows, LANES : 2 * LANES] = (cm * fc + sm * fs).astype(BF16)
            prod[1, rows, LANES : 2 * LANES] = (sm * fc - cm * fs).astype(BF16)
            uc = cm * cg + sm * sg
            us = sm * cg - cm * sg
            tc = twist[0, rows, :]
            ts = twist[1, rows, :]
            prod[0, rows, 2 * LANES :] = (uc * tc - us * ts).astype(BF16)
            prod[1, rows, 2 * LANES :] = (uc * ts + us * tc).astype(BF16)

        gain = skip[:, pl.ds(pl.multiple_of(me * chans + k * LANES, LANES), LANES)]

        def back(r, total):
            start = pl.multiple_of(r * rows_step, rows_step)
            rows = pl.ds(start, rows_step)
            y = jnp.dot(c4[rows, :], prod[0], preferred_element_type=F32)
            y = y + jnp.dot(s4[rows, :], prod[1], preferred_element_type=F32)
            y = y * (1.0 / length)
            gated = gx[k, rows, :LANES].astype(F32)
            grad = gx[k, rows, LANES:].astype(F32)
            gx[k, rows, :LANES] = y[:, :LANES].astype(BF16)
            gx[k, rows, LANES:] = (y[:, LANES : 2 * LANES] + gain * grad).astype(BF16)
            fgrad[k * LANES : (k + 1) * LANES, rows] = y[:, 2 * LANES :].T
            return total + jnp.sum(gated * grad, axis=0, keepdims=True)

        sgrad[:, k * LANES : (k + 1) * LANES] = lax.fori_loop(
            0, length // rows_step, back, jnp.zeros((1, LANES), F32)
        )
        to_peers(
            lambda peer: remote(
                gx.at[k, pl.ds(pl.multiple_of(peer * tokens, tokens), tokens), :],
                rx.at[k, me],
                r_send.at[k], r_recv.at[k], {"ctx": peer},
            )
        )
        rx[k, me] = gx[k, pl.ds(pl.multiple_of(me * tokens, tokens), tokens), :]

    def stage_d(k):
        drain(rx.at[k, pl.ds(0, groups - 1)], r_recv.at[k])
        drain(stg.at[k, pl.ds(0, groups - 1)], x_send.at[k])

        @pl.loop(0, groups)
        def _(group):
            query, keyed, value = features(k, group)
            gain = skip[:, pl.ds(column(0, group, k), LANES)]
            mixed = rx[k, group, :, :LANES].astype(F32)
            through = rx[k, group, :, LANES:].astype(F32)
            inner = mixed + gain * stg[k, group, :, :LANES].astype(F32)
            stg[k, group, :, :LANES] = (query * inner).astype(BF16)
            pltpu.make_async_copy(
                stg.at[k, group, :, pl.ds(0, LANES)],
                out.at[:, pl.ds(column(0, group, k), LANES)],
                o_sem.at[k],
            ).start()
            grads = (incv[k, group].astype(F32) * inner, through * value, through * keyed)
            for part in range(3):
                strip = part * groups + group
                grad = grads[part]
                fgb[strip, :tokens, :] = grad
                gst[k, strip] = grad[:HALO].astype(BF16)
                for j in range(taps):
                    kst[k, group, part, j : j + 1, :] = jnp.sum(
                        grad * xf[part, pl.ds(HALO - j, tokens), :], axis=0, keepdims=True
                    )
                kst[k, group, part, taps:, :] = jnp.zeros((8 - taps, LANES), F32)

        @pl.when(me > 0)
        def _():
            remote(gst.at[k], grx.at[k], g_send.at[k], g_recv.at[k], {"ctx": me - 1}).start()

        to_peers(
            lambda peer: remote(
                kst.at[k, peer], krx.at[k, me], ks_send.at[k], ks_recv.at[k], {"ctx": peer}
            )
        )
        krx[k, me] = kst[k, me]
        drain(krx.at[k, pl.ds(0, groups - 1)], ks_recv.at[k])
        total = krx[k, 0]
        for group in range(1, groups):
            total = total + krx[k, group]
        ksum[k] = total
        to_peers(
            lambda peer: remote(
                ksum.at[k], kall.at[k, me], ka_send.at[k], ka_recv.at[k], {"ctx": peer}
            )
        )
        kall[k, me] = total

        @pl.when(me < groups - 1)
        def _():
            drain(grx.at[k], g_recv.at[k])

        @pl.when(me == groups - 1)
        def _():
            grx[k] = jnp.zeros(grx.shape[1:], BF16)

        if k + 2 >= chunks:
            drain(srcv.at[k], src_send.at[k])
            drain(incv.at[k], inc_send.at[k])

        @pl.loop(0, groups)
        def _(group):
            for part in range(3):
                strip = part * groups + group
                fgb[strip, tokens:, :] = grx[k, strip].astype(F32)
                columns = pl.ds(column(part, group, k), LANES)
                total = None
                for j in range(taps):
                    term = kern[j : j + 1, columns] * fgb[strip, pl.ds(j, tokens), :]
                    total = term if total is None else total + term
                srcv[k, strip] = total.astype(BF16)
                pltpu.make_async_copy(
                    srcv.at[k, strip], igrad.at[:, columns], i_sem.at[k]
                ).start()

    for k in range(chunks):
        stage_a(k)
        if k > 0:
            stage_d(k - 1)
        stage_c(k)
    stage_d(chunks - 1)

    for k in range(chunks):
        drain(kall.at[k, pl.ds(0, groups - 1)], ka_recv.at[k])

        @pl.loop(0, groups)
        def _(group):
            for part in range(3):
                kgrad[:, pl.ds(column(part, group, k), LANES)] = kall[k, group, part, :taps, :]

        drain(srcv.at[k], i_sem.at[k])
        drain(srcv.at[k, pl.ds(0, groups)], o_sem.at[k])
        drain(gx.at[k, pl.ds(0, (groups - 1) * tokens), :], r_send.at[k])
        drain(kst.at[k, pl.ds(0, groups - 1)], ks_send.at[k])
        drain(kst.at[k, pl.ds(0, groups - 1)], ka_send.at[k])

        @pl.when(me < groups - 1)
        def _():
            drain(hst.at[k], h_send.at[k])

        @pl.when(me > 0)
        def _():
            drain(gst.at[k], g_send.at[k])


def on_device(sections, groups, acts, cots, kern, filt, skip):
    tokens, feats = acts.shape[1:]
    width = cots.shape[2]
    chans = width // groups
    chunks = chans // LANES
    length = filt.shape[2]
    taps = kern.shape[1]
    strips = 3 * groups
    vmem = pl.BlockSpec(memory_space=pltpu.VMEM)
    anywhere = pl.BlockSpec(memory_space=pl.ANY)
    dma = pltpu.SemaphoreType.DMA((chunks,))
    c4, s4, twist = make_tables(length)
    out, igrad, kgrad, fgrad, sgrad = pl.pallas_call(
        functools.partial(kernel, sections, groups, chunks),
        out_shape=(
            jax.ShapeDtypeStruct((tokens, width), BF16),
            jax.ShapeDtypeStruct((tokens, feats), BF16),
            jax.ShapeDtypeStruct((taps, feats), F32),
            jax.ShapeDtypeStruct((chans, length), F32),
            jax.ShapeDtypeStruct((1, chans), F32),
        ),
        in_specs=[anywhere, anywhere] + [vmem] * 6,
        out_specs=(anywhere, anywhere, vmem, vmem, vmem),
        scratch_shapes=[
            pltpu.VMEM((chunks, strips, tokens, LANES), BF16),
            pltpu.VMEM((chunks, groups, tokens, LANES), BF16),
            pltpu.VMEM((chunks, strips, HALO, LANES), BF16),
            pltpu.VMEM((chunks, strips, HALO, LANES), BF16),
            pltpu.VMEM((chunks, strips, HALO, LANES), BF16),
            pltpu.VMEM((chunks, strips, HALO, LANES), BF16),
            pltpu.VMEM((chunks, groups, tokens, 2 * LANES), BF16),
            pltpu.VMEM((chunks, length, 2 * LANES), BF16),
            pltpu.VMEM((chunks, groups, tokens, 2 * LANES), BF16),
            pltpu.VMEM((3, tokens + HALO, LANES), F32),
            pltpu.VMEM((strips, tokens + HALO, LANES), F32),
            pltpu.VMEM((2, chunks, length, LANES), BF16),
            pltpu.VMEM((2, length, 3 * LANES), BF16),
            pltpu.VMEM((chunks, groups, 3, 8, LANES), F32),
            pltpu.VMEM((chunks, groups, 3, 8, LANES), F32),
            pltpu.VMEM((chunks, 3, 8, LANES), F32),
            pltpu.VMEM((chunks, groups, 3, 8, LANES), F32),
        ]
        + [dma] * 18,
        compiler_params=pltpu.CompilerParams(
            collective_id=0, has_side_effects=True, vmem_limit_bytes=63 * 1024 * 1024
        ),
        cost_estimate=pl.CostEstimate(
            flops=2 * length * length * chans * 12, bytes_accessed=30_000_000, transcendentals=0
        ),
    )(acts[0], cots[0], kern[0], filt[0], skip, jnp.asarray(c4), jnp.asarray(s4), jnp.asarray(twist))
    return (out[None], igrad[None], kgrad[None], fgrad[None], sgrad)


def solution(mesh):
    return jax.shard_map(
        functools.partial(on_device, mesh.shape["section"], mesh.shape["ctx"]),
        mesh=mesh,
        in_specs=(
            P("section", "ctx", None),
            P("section", "ctx", None),
            P("section", None, None),
            P("section", "ctx", None),
            P("section", None),
        ),
        out_specs=(
            P("section", "ctx", None),
            P("section", "ctx", None),
            P("section", None, None),
            P("section", "ctx", None),
            P("section", "ctx"),
        ),
        check_vma=False,
    )
```

time: 625 us -> 200 us (0.32); the launches traced: 616 us -> 200 us
  other arithmetic: 223 us -> 0 us
  Pallas kernels: 0 us -> 187 us
  waiting for transfers between devices: 151 us -> 0 us
  matrix products: 76 us -> 0 us
  blocking collectives: 58.9 us -> 0 us
  local copies, waits for them, and re-layouts: 70.3 us -> 12.2 us
  starting transfers between devices: 21.3 us -> 0 us
  between operations: 14.9 us -> 0.64 us
    pallas_call x0 -> x1, Pallas kernels: none -> 187 us  [on_device(): pl.pallas_call(functools.partial(kernel, sections, groups, chunks), out_s...]
    dot_general x15 -> x0, matrix products: 76 us -> none  [the longest x9 63.6 us: contract(): return jnp.einsum(form, table, values, precision=lax.Precision.HIGH)]
    ppermute x4 -> x0, waiting for transfers between devices: 66.9 us -> none  [the longest x2 66.9 us: passed_along(): return lax.ppermute(value, axis, pairs)]
    all_to_all x2 -> x0, blocking collectives: 58.9 us -> none  [the longest x1 29.9 us: on_device(): lax.all_to_all(gated, 'ctx', split_axis=1, concat_axis=0, tiled=True)]
    unnamed x9 -> x0, other arithmetic: 52.7 us -> none
    add x5 -> x0, other arithmetic: 47.9 us -> none  [the longest x1 24.5 us: on_device(): sum((weights[offset][None, :] * padded[margin - offset:margin - offset +...]
    all_to_all x2 -> x0, waiting for transfers between devices: 44 us -> none  [the longest x1 24.4 us: on_device(): lax.all_to_all(mixed_part, 'ctx', split_axis=0, concat_axis=1, tiled=True)]
    psum x1 -> x0, waiting for transfers between devices: 40.4 us -> none  [on_device(): lax.psum(partial_kern.astype(jnp.bfloat16), 'ctx').astype(jnp.float32)]
  transfers between devices with their start and end apart: 7 -> 0, of which waited for: 4 -> 0; matrix products, arithmetic and copies ran while one was open for 22% -> 0% of each run, Pallas kernels for 0% -> 0%
where the time goes in v1:
time: 200 us
  Pallas kernels  187 us (94%)
  local copies, waits for them, and re-layouts  12.2 us (6%)
    pallas_call x1, Pallas kernels, on_device(): pl.pallas_call(functools.partial(kernel, sections, groups, chunks), out_s...  187 us
    unnamed x10, local copies, waits for them, and re-layouts  12.2 us

profile of v1, /device:TPU:0, one launch (start us, length us, event | category | flops | bytes accessed | tf_op | source)
XLA Modules:
  0.0 199.9 jit_solution(11906950861783981639)
XLA Ops:
  0.6 1.9 copy.16
  2.6 187.1 %shard_map.119 = (bf16[128,4096]{1,0:T(8,128)(2,1)}, bf16[128,12288]{1,0:T(8,128)(2,1)}, f32[7,12288]{1,0:T(8,128)}, f32[512,1024]{1,0:T(8,128)}, f32[1,512]{1,0:T(1,128)}) custom-call(bf16[128,12288]{1,0:T(8,128)(2,1)} %bitcast.15, bf16[128,4096]{1,0:T(8,128)(2,1)} %bitcast.16, f32[7,12288]{1,0:T(8,128)} %bitcast.14, bf16[512,1024]{1,0:T(8,128)(2,1)} %bitcast.17, ...), custom_call_target="tpu_custom_call" | custom-call | flops 12884901888 | bytes 30000000 | tf_op jit(solution)/shard_map/pallas_call | solution.py:337
  189.7 2.1 %copy.13 = f32[1,7,12288]{2,0,1:T(1,128)} copy(f32[1,7,12288]{2,1,0:T(8,128)} %bitcast.13) | data formatting | bytes 688128
  191.8 2.3 %copy.21 = bf16[1,128,4096]{2,1,0:T(8,128)(2,1)} copy(bf16[1,128,4096]{2,1,0:T(8,128)(2,1)} %bitcast.12) | data formatting | bytes 2097152
  194.1 0.0 copy-start
  194.1 4.0 %copy.22 = bf16[1,128,12288]{2,1,0:T(8,128)(2,1)} copy(bf16[1,128,12288]{2,1,0:T(8,128)(2,1)} %bitcast.10) | data formatting | bytes 6291456
  198.0 0.0 copy-done
  198.0 0.0 copy-start.1
  198.0 1.3 copy.23
  199.4 0.0 copy-done.1
  199.4 0.6 copy.24
Async XLA Ops:
  194.1 4.0 %copy-start = (f32[512,1024]{1,0:T(8,128)S(1)}, f32[512,1024]{1,0:T(8,128)}, u32[]{:S(2)}) copy-start(f32[512,1024]{1,0:T(8,128)} %get-tuple-element.13) | copy-start | bytes 6291460
  198.0 1.3 copy-start.1

commit v2 on v1

--- a/solution.py
+++ b/solution.py
@@ -101,14 +101,12 @@
             columns = pl.ds(column(part, group, k), LANES)
             total = None
             for j in range(taps):
-                term = kern[j : j + 1, columns] * xf[part, pl.ds(HALO - j, tokens), :]
+                term = kern[j, :, columns] * xf[part, pl.ds(HALO - j, tokens), :]
                 total = term if total is None else total + term
             result.append(total)
         return result
 
     hand_on(0)
-    if chunks > 1:
-        hand_on(1)
 
     @pl.loop(0, length // rows_step)
     def _(r):
@@ -126,10 +124,10 @@
 
     def stage_a(k):
         drain(srcv.at[k], src_recv.at[k])
-        if k + 2 < chunks:
-            drain(srcv.at[k], src_send.at[k])
-            drain(incv.at[k], inc_send.at[k])
-            hand_on(k + 2)
+        drain(srcv.at[k], src_send.at[k])
+        drain(incv.at[k], inc_send.at[k])
+        if k + 1 < chunks:
+            hand_on(k + 1)
 
         @pl.loop(0, 3 * groups)
         def _(strip):
@@ -253,6 +251,8 @@
             )
         )
         krx[k, me] = kst[k, me]
+
+    def stage_e(k):
         drain(krx.at[k, pl.ds(0, groups - 1)], ks_recv.at[k])
         total = krx[k, 0]
         for group in range(1, groups):
@@ -273,10 +273,6 @@
         def _():
             grx[k] = jnp.zeros(grx.shape[1:], BF16)
 
-        if k + 2 >= chunks:
-            drain(srcv.at[k], src_send.at[k])
-            drain(incv.at[k], inc_send.at[k])
-
         @pl.loop(0, groups)
         def _(group):
             for part in range(3):
@@ -285,19 +281,33 @@
                 columns = pl.ds(column(part, group, k), LANES)
                 total = None
                 for j in range(taps):
-                    term = kern[j : j + 1, columns] * fgb[strip, pl.ds(j, tokens), :]
+                    term = kern[j, :, columns] * fgb[strip, pl.ds(j, tokens), :]
                     total = term if total is None else total + term
                 srcv[k, strip] = total.astype(BF16)
                 pltpu.make_async_copy(
                     srcv.at[k, strip], igrad.at[:, columns], i_sem.at[k]
                 ).start()
 
+    plan = []
     for k in range(chunks):
-        stage_a(k)
-        if k > 0:
-            stage_d(k - 1)
-        stage_c(k)
-    stage_d(chunks - 1)
+        plan.append((stage_a, k))
+        if k == 0:
+            plan.append((stage_c, 0))
+        elif k == 1:
+            plan.append((stage_d, 0))
+        elif k == 2:
+            plan += [(stage_e, 0), (stage_c, 1)]
+        else:
+            plan += [(stage_c, k - 1), (stage_d, k - 2), (stage_e, k - 2)]
+    for k in range(chunks):
+        if (stage_c, k) not in plan:
+            plan.append((stage_c, k))
+    for k in range(chunks):
+        for stage in (stage_d, stage_e):
+            if (stage, k) not in plan:
+                plan.append((stage, k))
+    for stage, k in plan:
+        stage(k)
 
     for k in range(chunks):
         drain(kall.at[k, pl.ds(0, groups - 1)], ka_recv.at[k])
@@ -305,7 +315,9 @@
         @pl.loop(0, groups)
         def _(group):
             for part in range(3):
-                kgrad[:, pl.ds(column(part, group, k), LANES)] = kall[k, group, part, :taps, :]
+                columns = pl.ds(column(part, group, k), LANES)
+                for j in range(taps):
+                    kgrad[j, :, columns] = kall[k, group, part, j : j + 1, :]
 
         drain(srcv.at[k], i_sem.at[k])
         drain(srcv.at[k, pl.ds(0, groups)], o_sem.at[k])
@@ -320,6 +332,35 @@
         @pl.when(me > 0)
         def _():
             drain(gst.at[k], g_send.at[k])
+
+
+def copy_kernel(*refs):
+    count = len(refs) // 2
+    sems = refs[-1]
+    started = []
+    for i in range(count):
+        src, dst = refs[i], refs[count + i]
+        parts = 4 if src.shape[0] % 64 == 0 else 1
+        rows = src.shape[0] // parts
+        for part in range(parts):
+            here = pl.ds(part * rows, rows)
+            copy = pltpu.make_async_copy(src.at[here], dst.at[here], sems.at[i, part])
+            copy.start()
+            started.append(copy)
+    for copy in started:
+        copy.wait()
+
+
+def copied(arrays):
+    anywhere = pl.BlockSpec(memory_space=pl.ANY)
+    return pl.pallas_call(
+        copy_kernel,
+        out_shape=tuple(jax.ShapeDtypeStruct(a.shape, a.dtype) for a in arrays),
+        in_specs=[anywhere] * len(arrays),
+        out_specs=(anywhere,) * len(arrays),
+        scratch_shapes=[pltpu.SemaphoreType.DMA((len(arrays), 4))],
+        compiler_params=pltpu.CompilerParams(vmem_limit_bytes=63 * 1024 * 1024),
+    )(*arrays)
 
 
 def on_device(sections, groups, acts, cots, kern, filt, skip):
@@ -339,7 +380,7 @@
         out_shape=(
             jax.ShapeDtypeStruct((tokens, width), BF16),
             jax.ShapeDtypeStruct((tokens, feats), BF16),
-            jax.ShapeDtypeStruct((taps, feats), F32),
+            jax.ShapeDtypeStruct((taps, 1, feats), F32),
             jax.ShapeDtypeStruct((chans, length), F32),
             jax.ShapeDtypeStruct((1, chans), F32),
         ),
@@ -371,8 +412,9 @@
         cost_estimate=pl.CostEstimate(
             flops=2 * length * length * chans * 12, bytes_accessed=30_000_000, transcendentals=0
         ),
-    )(acts[0], cots[0], kern[0], filt[0], skip, jnp.asarray(c4), jnp.asarray(s4), jnp.asarray(twist))
-    return (out[None], igrad[None], kgrad[None], fgrad[None], sgrad)
+    )(acts[0], cots[0], kern.transpose(1, 0, 2), filt[0], skip, jnp.asarray(c4), jnp.asarray(s4), jnp.asarray(twist))
+    out, igrad, kgrad, fgrad = copied((out, igrad, kgrad, fgrad))
+    return (out[None], igrad[None], kgrad.transpose(1, 0, 2), fgrad[None], sgrad)
 
 
 def solution(mesh):

time: 200 us -> 373 us (1.86)
  Pallas kernels: 187 us -> 372 us
  local copies, waits for them, and re-layouts: 12.2 us -> 0.58 us
    pallas_call x0 -> x1, Pallas kernels: none -> 202 us  [copied(): pl.pallas_call(copy_kernel, out_shape=tuple((jax.ShapeDtypeStruct(a.shape...]
    pallas_call x1, Pallas kernels: 187 us -> 169 us  [on_device(): pl.pallas_call(functools.partial(kernel, sections, groups, chunks), out_s...]
    unnamed x10 -> x3, local copies, waits for them, and re-layouts: 12.2 us -> 0.58 us
where the time goes in v2:
time: 373 us
  Pallas kernels  372 us (100%)
    pallas_call x1, Pallas kernels, copied(): pl.pallas_call(copy_kernel, out_shape=tuple((jax.ShapeDtypeStruct(a.shape...  202 us
    pallas_call x1, Pallas kernels, on_device(): pl.pallas_call(functools.partial(kernel, sections, groups, chunks), out_s...  169 us

profile of v2, /device:TPU:0, one launch (start us, length us, event | category | flops | bytes accessed | tf_op | source)
XLA Modules:
  0.0 372.9 jit_solution(17142498794649648592)
XLA Ops:
  0.6 169.4 %shard_map.119 = (bf16[128,4096]{1,0:T(8,128)(2,1)}, bf16[128,12288]{1,0:T(8,128)(2,1)}, f32[7,1,12288]{2,1,0:T(1,128)}, f32[512,1024]{1,0:T(8,128)}, f32[1,512]{1,0:T(1,128)}) custom-call(bf16[128,12288]{1,0:T(8,128)(2,1)} %bitcast.8, bf16[128,4096]{1,0:T(8,128)(2,1)} %bitcast.11, f32[7,1,12288]{2,1,0:T(1,128)} %bitcast.14, bf16[512,1024]{1,0:T(8,128)(2,1)} %bitcast.12, ...), custom_call_target="tpu_custom_call" | custom-call | flops 12884901888 | bytes 30000000 | tf_op jit(solution)/shard_map/pallas_call | solution.py:378
  170.0 0.0 copy-start
  170.0 202.3 %shard_map.120 = (bf16[128,4096]{1,0:T(8,128)(2,1)}, bf16[128,12288]{1,0:T(8,128)(2,1)}, f32[7,1,12288]{2,1,0:T(1,128)}, f32[512,1024]{1,0:T(8,128)}) custom-call(bf16[128,4096]{1,0:T(8,128)(2,1)} %get-tuple-element.14.refs_0_, bf16[128,12288]{1,0:T(8,128)(2,1)} %get-tuple-element.15.refs_1_, f32[7,1,12288]{2,1,0:T(1,128)} %get-tuple-element.16.refs_2_, ...), custom_call_target="tpu_custom_call" | custom-call | tf_op jit(solution)/shard_map/pallas_call | solution.py:356
  372.3 0.0 copy-done
  372.3 0.6 copy.14
Async XLA Ops:
  170.0 202.3 %copy-start = (f32[1,512]{1,0:T(1,128)S(1)}, f32[1,512]{1,0:T(1,128)}, u32[]{:S(2)}) copy-start(f32[1,512]{1,0:T(1,128)} %get-tuple-element.32) | copy-start | bytes 6148

commit v3 on v2

--- a/solution.py
+++ b/solution.py
@@ -332,35 +332,6 @@
         @pl.when(me > 0)
         def _():
             drain(gst.at[k], g_send.at[k])
-
-
-def copy_kernel(*refs):
-    count = len(refs) // 2
-    sems = refs[-1]
-    started = []
-    for i in range(count):
-        src, dst = refs[i], refs[count + i]
-        parts = 4 if src.shape[0] % 64 == 0 else 1
-        rows = src.shape[0] // parts
-        for part in range(parts):
-            here = pl.ds(part * rows, rows)
-            copy = pltpu.make_async_copy(src.at[here], dst.at[here], sems.at[i, part])
-            copy.start()
-            started.append(copy)
-    for copy in started:
-        copy.wait()
-
-
-def copied(arrays):
-    anywhere = pl.BlockSpec(memory_space=pl.ANY)
-    return pl.pallas_call(
-        copy_kernel,
-        out_shape=tuple(jax.ShapeDtypeStruct(a.shape, a.dtype) for a in arrays),
-        in_specs=[anywhere] * len(arrays),
-        out_specs=(anywhere,) * len(arrays),
-        scratch_shapes=[pltpu.SemaphoreType.DMA((len(arrays), 4))],
-        compiler_params=pltpu.CompilerParams(vmem_limit_bytes=63 * 1024 * 1024),
-    )(*arrays)
 
 
 def on_device(sections, groups, acts, cots, kern, filt, skip):
@@ -413,7 +384,6 @@
             flops=2 * length * length * chans * 12, bytes_accessed=30_000_000, transcendentals=0
         ),
     )(acts[0], cots[0], kern.transpose(1, 0, 2), filt[0], skip, jnp.asarray(c4), jnp.asarray(s4), jnp.asarray(twist))
-    out, igrad, kgrad, fgrad = copied((out, igrad, kgrad, fgrad))
     return (out[None], igrad[None], kgrad.transpose(1, 0, 2), fgrad[None], sgrad)
 
 

time: 373 us -> 179 us (0.48)
  Pallas kernels: 372 us -> 169 us
  local copies, waits for them, and re-layouts: 0.58 us -> 8.91 us
    pallas_call x1 -> x0, Pallas kernels: 202 us -> none  [copied(): pl.pallas_call(copy_kernel, out_shape=tuple((jax.ShapeDtypeStruct(a.shape...]
    unnamed x3 -> x11, local copies, waits for them, and re-layouts: 0.58 us -> 8.91 us
where the time goes in v3:
time: 179 us
  Pallas kernels  169 us (94%)
  local copies, waits for them, and re-layouts  8.91 us (5%)
    pallas_call x1, Pallas kernels, on_device(): pl.pallas_call(functools.partial(kernel, sections, groups, chunks), out_s...  169 us
    unnamed x11, local copies, waits for them, and re-layouts  8.91 us

profile of v3, /device:TPU:0, one launch (start us, length us, event | category | flops | bytes accessed | tf_op | source)
XLA Modules:
  0.0 178.9 jit_solution(9587326237215563251)
XLA Ops:
  0.6 169.4 %shard_map.119 = (bf16[128,4096]{1,0:T(8,128)(2,1)}, bf16[128,12288]{1,0:T(8,128)(2,1)}, f32[7,1,12288]{2,1,0:T(1,128)}, f32[512,1024]{1,0:T(8,128)}, f32[1,512]{1,0:T(1,128)}) custom-call(bf16[128,12288]{1,0:T(8,128)(2,1)} %bitcast.12, bf16[128,4096]{1,0:T(8,128)(2,1)} %bitcast.13, f32[7,1,12288]{2,1,0:T(1,128)} %bitcast.15, bf16[512,1024]{1,0:T(8,128)(2,1)} %bitcast.14, ...), custom_call_target="tpu_custom_call" | custom-call | flops 12884901888 | bytes 30000000 | tf_op jit(solution)/shard_map/pallas_call | solution.py:349
  170.0 2.3 %copy.18 = bf16[1,128,4096]{2,1,0:T(8,128)(2,1)} copy(bf16[1,128,4096]{2,1,0:T(8,128)(2,1)} %bitcast.10) | data formatting | bytes 2097152
  172.3 0.0 copy-start.1
  172.3 0.0 copy-start
  172.3 4.0 %copy.19 = bf16[1,128,12288]{2,1,0:T(8,128)(2,1)} copy(bf16[1,128,12288]{2,1,0:T(8,128)(2,1)} %bitcast.8) | data formatting | bytes 6291456
  176.3 0.0 copy-done.1
  176.3 0.7 copy.20
  177.0 0.0 copy-done
  177.0 0.0 copy-start.2
  177.0 1.3 copy.21
  178.3 0.0 copy-done.2
  178.3 0.6 copy.22
Async XLA Ops:
  172.3 4.0 %copy-start.1 = (f32[7,1,12288]{2,1,0:T(1,128)S(1)}, f32[7,1,12288]{2,1,0:T(1,128)}, u32[]{:S(2)}) copy-start(f32[7,1,12288]{2,1,0:T(1,128)} %get-tuple-element.12) | copy-start | bytes 1032196
  172.3 4.7 %copy-start = (f32[512,1024]{1,0:T(8,128)S(1)}, f32[512,1024]{1,0:T(8,128)}, u32[]{:S(2)}) copy-start(f32[512,1024]{1,0:T(8,128)} %get-tuple-element.13) | copy-start | bytes 6291460
  177.0 1.3 copy-start.2
